TPU v7x, 32 devices: a whole 2x2x4 slice. The times are simulated.
32 devices in a mesh: slab: 4 (over z), region: 8 (over y, x, core).
Axes of the slice: x: 2, y: 2, z: 4, core: 2. Of those that a mesh axis runs over, the one named last changes fastest.
Arguments:
- prior_matrix: float32 [256, 65536], P('region', 'slab'), may hold values from -6 to 6
- prior_at_measurements: float32 [256, 8192], P('region', 'slab'), may hold values from -6 to 6
- scaled_residual_vector: float32 [256, 8192], P('region', 'slab'), may hold values from -6 to 6
- lattice_coordinates: float32 [2, 65536], P(None, 'slab'), may hold values from 0 to 2
- measurement_coordinates: float32 [2, 8192], replicated, may hold values from 0 to 2
- neighbour_block_totals: int32 [512], P('slab'), may hold values from 2 to 16, as said below
- neighbour_block_numbers: int32 [512, 16], P('slab'), may hold values from 0 to 19, as said below
Outputs:
- analysis: float32 [256, 65536], P('region', 'slab')
Inputs may be any that keep to these rules, and one draw needn't show every extreme that they name: neighbour_block_totals[t] observation tiles are listed for grid tile t; in every slab some grid tile lists 16 and some lists 2. `neighbour_block_numbers`: row t's first neighbour_block_totals[t] entries are distinct, and each names an observation tile s * 16 - 2 + e that exists (from 0 to 16 * 4 - 1), s being t's slab; the remaining entries of the row are 0.
All inputs are finite; a program needn't handle non-finite values.
Results may differ from a plain program's by a relative error of at most 0.0003.
Values sent between devices are 32-bit elements; how exact they have to be, the bound alone decides.
A program may use at most 64 MiB of HBM per device.

v0:
```python
import functools

import jax
import jax.numpy as jnp
from jax import lax
from jax.experimental import pallas as pl
from jax.experimental.pallas import tpu as pltpu
from jax.sharding import PartitionSpec as P

TILE = 128
EDGE = 2
GROUP = 4
PARTS = 4
MESH = pl.DeviceIdType.MESH


def flip(index, bits):
    step = 1
    while step <= bits:
        if bits & step:
            index = index + step - 2 * step * ((index // step) % 2)
        step *= 2
    return index


def push(src, dst, send, recv, slab, region):
    copy = pltpu.make_async_remote_copy(
        src_ref=src,
        dst_ref=dst,
        send_sem=send,
        recv_sem=recv,
        device_id=(slab, region),
        device_id_type=MESH,
    )
    copy.start()
    return copy


def ensemble_kernel(
    n,
    slabs,
    parts,
    totals,
    numbers,
    prior,
    obs,
    res,
    gxy,
    oxy,
    back,
    fore,
    increment,
    obs_all,
    res_all,
    ot,
    rr,
    ox,
    oy,
    tapers,
    ff,
    held,
    own_sem,
    fore_send,
    fore_recv,
    near_send,
    near_recv,
    edge_send,
    edge_recv,
    back_send,
    back_recv,
):
    slab = lax.axis_index("slab")
    region = lax.axis_index("region")
    mine, points = obs.shape
    groups, slots = prior.shape[:2]
    most = numbers.shape[0]
    members = mine * n
    part = slots // parts
    steps = most // GROUP
    obs_tiles = obs_all.shape[1] // TILE
    scale = 1.0 / (members - 1.0)
    margin = EDGE * TILE
    sources = (obs, res)
    targets = (obs_all, res_all)
    above = slab < slabs - 1
    below = slab > 0

    def rows(owner):
        return pl.ds(pl.multiple_of(owner * mine, 8), mine)

    def fore_rows(owner):
        return pl.ds(owner * groups, groups)

    middle = pl.ds(margin, points)
    low = pl.ds(0, margin)
    high = pl.ds(margin + points, margin)

    barrier = pltpu.get_barrier_semaphore()
    for k in range(1, n):
        pl.semaphore_signal(
            barrier, inc=1, device_id=(slab, flip(region, k)), device_id_type=MESH
        )

    for exists, other in ((above, slab + 1), (below, slab - 1)):

        @pl.when(exists)
        def _(other=other):
            for k in (0, 1):
                pl.semaphore_signal(
                    barrier, inc=1, device_id=(other, flip(region, k)), device_id_type=MESH
                )

    beside = above.astype(jnp.int32) + below.astype(jnp.int32)
    pl.semaphore_wait(barrier, n - 1 + 2 * beside)

    def edge_copies(k, side, other, act):
        block = rows(flip(region, k))
        for a in range(2):
            if k == 0:
                src = sources[a].at[:, pl.ds(points - margin, margin) if side == 0 else low]
            else:
                first = points if side == 0 else margin
                src = targets[a].at[block, pl.ds(first, margin)]
            for core in range(2):
                copy = pltpu.make_async_remote_copy(
                    src_ref=src,
                    dst_ref=targets[a].at[block, low if side == 0 else high],
                    send_sem=edge_send.at[side, a, k + core],
                    recv_sem=edge_recv.at[side, a, k + core],
                    device_id=(other, flip(region, core)),
                    device_id_type=MESH,
                )
                act(copy)

    def send_edges(k):
        for side, exists, other in ((0, above, slab + 1), (1, below, slab - 1)):

            @pl.when(exists)
            def _(side=side, other=other):
                edge_copies(k, side, other, lambda copy: copy.start())

    sent = []
    bits = [1 << b for b in range(1, n.bit_length() - 1)]

    def forward(k):
        for a in range(2):
            place = targets[a].at[rows(flip(region, k)), middle]
            src = sources[a] if k == 0 else place
            for bit in bits:
                to = k | bit
                last = [b for b in bits if b & to][-1 if a == 0 else 0]
                if k & bit or last != bit:
                    continue
                sent.append(
                    push(
                        src,
                        place,
                        near_send.at[a, to],
                        near_recv.at[a, to],
                        slab,
                        flip(region, bit),
                    )
                )
            sent.append(
                push(src, place, near_send.at[a, k + 1], near_recv.at[a, k + 1], slab, flip(region, 1))
            )

    def near_wait(a, k):
        place = targets[a].at[rows(flip(region, k)), middle]
        pltpu.make_async_copy(place, place, near_recv.at[a, k]).wait()

    def send_fore():
        for g in range(parts):
            some = pl.ds(g * part, part)
            for k in [*range(2, n), 1]:
                sent.append(
                    push(
                        prior.at[:, some, flip(region, k)],
                        fore.at[fore_rows(region), some],
                        fore_send.at[g, k],
                        fore_recv.at[g, k],
                        slab,
                        flip(region, k),
                    )
                )

    last_tile = oxy.shape[1] // TILE - 1
    first_tile = slab * (points // TILE) - EDGE

    def spread(q, carry):
        place = jnp.clip(first_tile + q, 0, last_tile)
        there = pl.ds(pl.multiple_of(place * TILE, TILE), TILE)
        ox[q] = jnp.broadcast_to(oxy[0:1, there], (TILE, TILE)).T
        oy[q] = jnp.broadcast_to(oxy[1:2, there], (TILE, TILE)).T
        return carry

    def taper_slot(slot, carry):
        tile = slot * n + region
        columns = pl.ds(pl.multiple_of(tile * TILE, TILE), TILE)
        gx = gxy[0:1, columns]
        gy = gxy[1:2, columns]
        count = totals[tile]

        def one(p, inner):
            q = numbers[p, tile]
            away = jnp.where(p < count, 0.0, 64.0)
            tapers[slot * most + p] = taper_of(gx + away, gy, ox[q], oy[q])
            return inner

        return lax.fori_loop(0, most, one, carry)

    forward(0)
    send_edges(0)
    own = [
        pltpu.make_async_copy(sources[a], targets[a].at[rows(region), middle], own_sem.at[a])
        for a in range(2)
    ]
    own.append(pltpu.make_async_copy(prior.at[:, :, region], fore.at[fore_rows(region)], own_sem.at[2]))
    for copy in own:
        copy.start()

    for exists, columns in ((below, low), (above, high)):

        @pl.when(jnp.logical_not(exists))
        def _(columns=columns):
            for a in range(2):
                targets[a][:, columns] = jnp.zeros((members, margin), jnp.float32)

    half, most_of = slots // 2, 3 * slots // 4
    lax.fori_loop(0, obs_tiles, spread, 0)
    lax.fori_loop(0, half, taper_slot, 0)
    even = sorted(range(2, n, 2), key=lambda k: (k.bit_count(), k))
    single = [k for k in even if k.bit_count() == 1]
    for k in even:
        for a in range(2):
            near_wait(a, k)
        forward(k)
        send_edges(k)
        if k == single[-1]:
            lax.fori_loop(half, most_of, taper_slot, 0)
    send_fore()
    lax.fori_loop(most_of, slots, taper_slot, 0)

    for k in range(1, n, 2):
        for a in range(2):
            near_wait(a, k)
    for side, comes in ((0, below), (1, above)):

        @pl.when(comes)
        def _(side=side):
            for k in range(n):
                for a in range(2):
                    place = targets[a].at[rows(flip(region, k)), low if side == 0 else high]
                    pltpu.make_async_copy(place, place, edge_recv.at[side, a, k]).wait()

    for copy in own[:2]:
        copy.wait()

    def prepare(q, carry):
        columns = pl.ds(pl.multiple_of(q * TILE, TILE), TILE)
        values = obs_all[:, columns]
        values = values - jnp.mean(values, axis=0, keepdims=True)
        high, low = split(values.T)
        ot[q, :TILE, :] = high
        ot[q, TILE:, :] = low
        high, low = split(res_all[:, columns])
        rr[q, :, :TILE] = high
        rr[q, :, TILE:] = low
        return carry

    lax.fori_loop(0, obs_tiles, prepare, 0)
    own[2].wait()

    def prepare_fore(slot, carry):
        values = fore[:, slot].reshape(members, TILE)
        values = (values - jnp.mean(values, axis=0, keepdims=True)) * scale
        high, low = split(values)
        ff[slot, :, :TILE] = high
        ff[slot, :, TILE:] = low
        increment[:, slot] = jnp.zeros((members // 8, 8, TILE), jnp.float32)
        return carry

    def spend(slot, step):
        tile = slot * n + region
        found = [numbers[step * GROUP + k, tile] for k in range(GROUP)]
        weights = held[...]
        both = dot(jnp.concatenate([rr[q, :, :TILE] for q in found], axis=1), weights)
        rest = dot(jnp.concatenate([rr[q, :, TILE:] for q in found], axis=1), weights[:, :TILE])
        return both[:, :TILE] + (both[:, TILE:] + rest)

    def store(slot, term):
        increment[:, slot] += term.reshape(members // 8, 8, TILE)

    for g in range(parts):
        some = pl.ds(g * part, part)
        for k in range(1, n):
            place = fore.at[fore_rows(flip(region, k)), some]
            pltpu.make_async_copy(place, place, fore_recv.at[g, k]).wait()
        lax.fori_loop(g * part, (g + 1) * part, prepare_fore, 0)
        held[...] = jnp.zeros_like(held)

        def body(turn, carry, start=g * part):
            slot = start + turn // steps
            step = turn % steps
            before = jnp.maximum(turn - 1, 0)
            old = start + before // steps
            term = spend(old, before % steps)
            tile = slot * n + region
            made = []
            for k in range(GROUP):
                p = step * GROUP + k
                q = numbers[p, tile]
                four = dot(ot[q], ff[slot])
                covariance = four[:TILE, :TILE] + (four[:TILE, TILE:] + four[TILE:, :TILE])
                made.append(split(tapers[slot * most + p] * covariance))
            for k in range(GROUP):
                held[k * TILE : (k + 1) * TILE, :TILE] = made[k][0]
                held[k * TILE : (k + 1) * TILE, TILE:] = made[k][1]
            store(old, term)
            return carry

        lax.fori_loop(0, part * steps, body, 0)
        store((g + 1) * part - 1, spend((g + 1) * part - 1, steps - 1))
        for k in [*range(2, n), 1]:
            other = flip(region, k)
            sent.append(
                push(
                    increment.at[fore_rows(other), some],
                    back.at[:, some, region],
                    back_send.at[g, k],
                    back_recv.at[g, k],
                    slab,
                    other,
                )
            )
        own.append(
            pltpu.make_async_copy(
                increment.at[fore_rows(region), some], back.at[:, some, region], own_sem.at[3 + g]
            )
        )
        own[-1].start()

    for g in range(parts):
        for k in range(1, n):
            place = back.at[:, pl.ds(g * part, part), flip(region, k)]
            pltpu.make_async_copy(place, place, back_recv.at[g, k]).wait()

    for side, exists, other in ((0, above, slab + 1), (1, below, slab - 1)):

        @pl.when(exists)
        def _(side=side, other=other):
            for k in range(0, n, 2):
                edge_copies(k, side, other, lambda copy: copy.wait_send())

    for copy in sent:
        copy.wait_send()
    for copy in own[3:]:
        copy.wait()


def analyse(n, slabs, totals, numbers, prior, obs, res, gxy, oxy):
    groups, slots = prior.shape[:2]
    mine, points = obs.shape
    most = numbers.shape[0]
    members = mine * n
    parts = PARTS if slots % PARTS == 0 else 1
    obs_tiles = points // TILE + 2 * EDGE
    wide = pltpu.VMEM((members, points + 2 * EDGE * TILE), jnp.float32)
    tiles = pltpu.VMEM((groups * n, slots, 8, TILE), jnp.float32)
    spread = pltpu.VMEM((obs_tiles, TILE, TILE), jnp.float32)
    smem = pl.BlockSpec(memory_space=pltpu.SMEM)
    vmem = pl.BlockSpec(memory_space=pltpu.VMEM)
    hbm = pl.BlockSpec(memory_space=pltpu.HBM)
    dma = pltpu.SemaphoreType.DMA
    return pl.pallas_call(
        functools.partial(ensemble_kernel, n, slabs, parts),
        out_shape=jax.ShapeDtypeStruct((groups, slots, n, 8, TILE), jnp.float32),
        in_specs=[smem, smem, hbm, hbm, hbm, vmem, vmem],
        out_specs=pl.BlockSpec(memory_space=pl.ANY),
        scratch_shapes=[
            tiles,
            tiles,
            wide,
            wide,
            pltpu.VMEM((obs_tiles, 2 * TILE, members), jnp.bfloat16),
            pltpu.VMEM((obs_tiles, members, 2 * TILE), jnp.bfloat16),
            spread,
            spread,
            pltpu.VMEM((slots * most, TILE, TILE), jnp.float32),
            pltpu.VMEM((slots, members, 2 * TILE), jnp.bfloat16),
            pltpu.VMEM((GROUP * TILE, 2 * TILE), jnp.bfloat16),
            dma((3 + parts,)),
            dma((parts, n)),
            dma((parts, n)),
            dma((2, n)),
            dma((2, n)),
            dma((2, 2, n)),
            dma((2, 2, n)),
            dma((parts, n)),
            dma((parts, n)),
        ],
        compiler_params=pltpu.CompilerParams(
            collective_id=0, has_side_effects=True, vmem_limit_bytes=50 * 1024 * 1024
        ),
    )(totals, numbers, prior, obs, res, gxy, oxy)


def split(x):
    high = x.astype(jnp.bfloat16)
    low = (x - high.astype(jnp.float32)).astype(jnp.bfloat16)
    return high, low


def taper_of(gx, gy, ox, oy):
    dx = ox - gx
    dy = oy - gy
    d2 = dx * dx + dy * dy
    inv = lax.rsqrt(jnp.maximum(d2, 1e-30))
    z = d2 * inv
    a = 0.5 * d2 - 5.0 / 3.0
    near = d2 * (z * (0.625 - 0.25 * d2) + a) + 1.0
    far = d2 * (z * (0.625 + d2 * (1.0 / 12.0)) - a) + (4.0 - 5.0 * z) - (2.0 / 3.0) * inv
    return jnp.where(d2 <= 1.0, near, jnp.where(d2 <= 4.0, far, 0.0))


def dot(a, b):
    return lax.dot_general(a, b, (((1,), (0,)), ((), ())), preferred_element_type=jnp.float32)


def per_device(
    prior_matrix,
    prior_at_measurements,
    scaled_residual_vector,
    lattice_coordinates,
    measurement_coordinates,
    neighbour_block_totals,
    neighbour_block_numbers,
):
    regions = lax.axis_size("region")
    mine, points = prior_matrix.shape
    slots = neighbour_block_totals.shape[0] // regions
    blocks = prior_matrix.reshape(mine // 8, 8, slots, regions, TILE).transpose(0, 2, 3, 1, 4)
    back = analyse(
        regions,
        lax.axis_size("slab"),
        neighbour_block_totals,
        neighbour_block_numbers.T,
        blocks,
        prior_at_measurements,
        scaled_residual_vector,
        lattice_coordinates,
        measurement_coordinates,
    )
    return prior_matrix + back.transpose(0, 3, 1, 2, 4).reshape(mine, points)


def solution(mesh):
    in_specs = (
        P("region", "slab"),
        P("region", "slab"),
        P("region", "slab"),
        P(None, "slab"),
        P(),
        P("slab"),
        P("slab", None),
    )
    return jax.shard_map(
        per_device, mesh=mesh, in_specs=in_specs, out_specs=P("region", "slab"), check_vma=False
    )
```

profile of v0, /device:TPU:0, one launch (start us, length us, event | category | flops | bytes accessed | tf_op | source)
XLA Modules:
  0.0 81.3 jit_solution(15721823865132102747)
XLA Ops:
  0.0 0.0 copy-start
  0.0 0.9 %copy-done = f32[32,2048]{1,0:T(8,128)S(1)} copy-done((f32[32,2048]{1,0:T(8,128)S(1)}, f32[32,2048]{1,0:T(8,128)}, u32[]{:S(2)}) %copy-start) | copy-done | bytes 262168
  1.0 0.0 copy-start.1
  1.0 0.9 %copy-done.1 = f32[32,2048]{1,0:T(8,128)S(1)} copy-done((f32[32,2048]{1,0:T(8,128)S(1)}, f32[32,2048]{1,0:T(8,128)}, u32[]{:S(2)}) %copy-start.1) | copy-done | bytes 262168
  1.9 0.0 copy-start.2
  1.9 0.9 %copy-done.2 = f32[2,16384]{1,0:T(2,128)S(1)} copy-done((f32[2,16384]{1,0:T(2,128)S(1)}, f32[2,16384]{1,0:T(2,128)}, u32[]{:S(2)}) %copy-start.2) | copy-done | bytes 131096
  2.8 0.0 copy-start.3
  2.8 0.8 %copy-done.3 = f32[2,8192]{1,0:T(2,128)S(1)} copy-done((f32[2,8192]{1,0:T(2,128)S(1)}, f32[2,8192]{1,0:T(2,128)}, u32[]{:S(2)}) %copy-start.3) | copy-done | bytes 65560
  3.6 0.0 copy-start.4
  3.6 0.7 copy-done.4
  4.3 0.0 copy-start.5
  4.3 0.7 copy-done.5
  5.0 0.0 copy-start.6
  5.0 74.7 %shard_map.73 = f32[4,16,8,8,128]{4,3,2,1,0:T(8,128)S(1)} custom-call(s32[128]{0:T(128)S(1)} %copy-done.5, s32[16,128]{1,0:T(8,128)S(1)} %bitcast.8, f32[4,16,8,8,128]{4,3,2,1,0:T(8,128)} %bitcast.9, f32[32,2048]{1,0:T(8,128)S(1)} %copy-done, f32[32,2048]{1,0:T(8,128)S(1)} %copy-done.1, f32[2,16384]{1,0:T(2,128)S(1)} %copy-done.2, f32[2,8192]{1,0:T(2,128)S(1)} %copy-done.3), custom_call_target="tpu_custom_call" | custom-call | tf_op jit(solution)/shard_map/pallas_call | solution.py:375
  79.7 0.0 copy-done.6
  79.7 1.5 %add.3 = f32[32,16384]{1,0:T(8,128)} add(f32[32,16384]{1,0:T(8,128)S(1)} %copy-done.6, f32[32,16384]{1,0:T(8,128)S(1)} %bitcast.7) | non-fusion elementwise | flops 524288 | bytes 6291456 | tf_op jit(solution)/shard_map/add | solution.py:454
Async XLA Ops:
  0.0 0.9 %copy-start = (f32[32,2048]{1,0:T(8,128)S(1)}, f32[32,2048]{1,0:T(8,128)}, u32[]{:S(2)}) copy-start(f32[32,2048]{1,0:T(8,128)} %obs.1) | copy-start | bytes 786436
  1.0 0.9 %copy-start.1 = (f32[32,2048]{1,0:T(8,128)S(1)}, f32[32,2048]{1,0:T(8,128)}, u32[]{:S(2)}) copy-start(f32[32,2048]{1,0:T(8,128)} %res.1) | copy-start | bytes 786436
  1.9 0.9 %copy-start.2 = (f32[2,16384]{1,0:T(2,128)S(1)}, f32[2,16384]{1,0:T(2,128)}, u32[]{:S(2)}) copy-start(f32[2,16384]{1,0:T(2,128)} %gxy.1) | copy-start | bytes 393220
  2.8 0.8 %copy-start.3 = (f32[2,8192]{1,0:T(2,128)S(1)}, f32[2,8192]{1,0:T(2,128)}, u32[]{:S(2)}) copy-start(f32[2,8192]{1,0:T(2,128)} %oxy.1) | copy-start | bytes 196612
  3.6 0.7 copy-start.4
  4.3 0.7 copy-start.5
  5.0 74.7 %copy-start.6 = (f32[32,16384]{1,0:T(8,128)S(1)}, f32[32,16384]{1,0:T(8,128)}, u32[]{:S(2)}) copy-start(f32[32,16384]{1,0:T(8,128)} %param.7) | copy-start | bytes 6291460
where the time goes:
time: 81.6 us; the launch traced here: 81.3 us
  Pallas kernels  74.7 us (92%)
  local copies, waits for them, and re-layouts  5 us (6%)
  other arithmetic  1.53 us (2%)
    pallas_call x1, Pallas kernels, analyse(): pl.pallas_call(functools.partial(ensemble_kernel, n, slabs, parts), out_s...  74.7 us
    unnamed x14, local copies, waits for them, and re-layouts  5 us

commit v1 on v0

--- a/solution.py
+++ b/solution.py
@@ -45,9 +45,11 @@
     prior,
     obs,
     res,
+    gxy_all,
+    oxy_all,
+    back,
     gxy,
     oxy,
-    back,
     fore,
     increment,
     obs_all,
@@ -95,6 +97,13 @@
     low = pl.ds(0, margin)
     high = pl.ds(margin + points, margin)
 
+    places = [
+        pltpu.make_async_copy(gxy_all, gxy, own_sem.at[3 + parts]),
+        pltpu.make_async_copy(oxy_all, oxy, own_sem.at[4 + parts]),
+    ]
+    for copy in places:
+        copy.start()
+
     barrier = pltpu.get_barrier_semaphore()
     for k in range(1, n):
         pl.semaphore_signal(
@@ -227,6 +236,8 @@
                 targets[a][:, columns] = jnp.zeros((members, margin), jnp.float32)
 
     half, most_of = slots // 2, 3 * slots // 4
+    for copy in places:
+        copy.wait()
     lax.fori_loop(0, obs_tiles, spread, 0)
     lax.fori_loop(0, half, taper_slot, 0)
     even = sorted(range(2, n, 2), key=lambda k: (k.bit_count(), k))
@@ -284,9 +295,17 @@
         tile = slot * n + region
         found = [numbers[step * GROUP + k, tile] for k in range(GROUP)]
         weights = held[...]
-        both = dot(jnp.concatenate([rr[q, :, :TILE] for q in found], axis=1), weights)
-        rest = dot(jnp.concatenate([rr[q, :, TILE:] for q in found], axis=1), weights[:, :TILE])
-        return both[:, :TILE] + (both[:, TILE:] + rest)
+        both = dot(
+            jnp.concatenate(
+                [
+                    jnp.concatenate([rr[q, :, :TILE] for q in found], axis=1),
+                    jnp.concatenate([rr[q, :, TILE:] for q in found], axis=1),
+                ],
+                axis=0,
+            ),
+            weights,
+        )
+        return both[:members, :TILE] + (both[:members, TILE:] + both[members:, :TILE])
 
     def store(slot, term):
         increment[:, slot] += term.reshape(members // 8, 8, TILE)
@@ -307,10 +326,11 @@
             term = spend(old, before % steps)
             tile = slot * n + region
             made = []
+            listed = [ot[numbers[step * GROUP + k, tile]] for k in range(GROUP)]
+            every = dot(jnp.concatenate(listed, axis=0), ff[slot])
             for k in range(GROUP):
                 p = step * GROUP + k
-                q = numbers[p, tile]
-                four = dot(ot[q], ff[slot])
+                four = every[2 * TILE * k : 2 * TILE * (k + 1)]
                 covariance = four[:TILE, :TILE] + (four[:TILE, TILE:] + four[TILE:, :TILE])
                 made.append(split(tapers[slot * most + p] * covariance))
             for k in range(GROUP):
@@ -369,15 +389,16 @@
     tiles = pltpu.VMEM((groups * n, slots, 8, TILE), jnp.float32)
     spread = pltpu.VMEM((obs_tiles, TILE, TILE), jnp.float32)
     smem = pl.BlockSpec(memory_space=pltpu.SMEM)
-    vmem = pl.BlockSpec(memory_space=pltpu.VMEM)
     hbm = pl.BlockSpec(memory_space=pltpu.HBM)
     dma = pltpu.SemaphoreType.DMA
     return pl.pallas_call(
         functools.partial(ensemble_kernel, n, slabs, parts),
         out_shape=jax.ShapeDtypeStruct((groups, slots, n, 8, TILE), jnp.float32),
-        in_specs=[smem, smem, hbm, hbm, hbm, vmem, vmem],
+        in_specs=[smem, smem, hbm, hbm, hbm, hbm, hbm],
         out_specs=pl.BlockSpec(memory_space=pl.ANY),
         scratch_shapes=[
+            pltpu.VMEM(gxy.shape, jnp.float32),
+            pltpu.VMEM(oxy.shape, jnp.float32),
             tiles,
             tiles,
             wide,
@@ -389,7 +410,7 @@
             pltpu.VMEM((slots * most, TILE, TILE), jnp.float32),
             pltpu.VMEM((slots, members, 2 * TILE), jnp.bfloat16),
             pltpu.VMEM((GROUP * TILE, 2 * TILE), jnp.bfloat16),
-            dma((3 + parts,)),
+            dma((5 + parts,)),
             dma((parts, n)),
             dma((parts, n)),
             dma((2, n)),
@@ -400,7 +421,7 @@
             dma((parts, n)),
         ],
         compiler_params=pltpu.CompilerParams(
-            collective_id=0, has_side_effects=True, vmem_limit_bytes=50 * 1024 * 1024
+            collective_id=0, has_side_effects=True, vmem_limit_bytes=62 * 1024 * 1024
         ),
     )(totals, numbers, prior, obs, res, gxy, oxy)
 
@@ -417,10 +438,11 @@
     d2 = dx * dx + dy * dy
     inv = lax.rsqrt(jnp.maximum(d2, 1e-30))
     z = d2 * inv
-    a = 0.5 * d2 - 5.0 / 3.0
-    near = d2 * (z * (0.625 - 0.25 * d2) + a) + 1.0
-    far = d2 * (z * (0.625 + d2 * (1.0 / 12.0)) - a) + (4.0 - 5.0 * z) - (2.0 / 3.0) * inv
-    return jnp.where(d2 <= 1.0, near, jnp.where(d2 <= 4.0, far, 0.0))
+    near = d2 * (z * (0.625 - 0.25 * d2) + (0.5 * d2 - 5.0 / 3.0)) + 1.0
+    rest = jnp.maximum(2.0 - z, 0.0)
+    square = rest * rest
+    far = (square * square) * (z * (z * (1.0 / 12.0) + 1.0 / 6.0) - 1.0 / 24.0) * inv
+    return jnp.where(d2 <= 1.0, near, far)
 
 
 def dot(a, b):

time: 81.6 us -> 80.4 us (0.985)
  local copies, waits for them, and re-layouts: 5 us -> 0 us
  other arithmetic: 1.53 us -> 3.75 us
  Pallas kernels: 74.7 us -> 76.4 us
    unnamed x14 -> x0, local copies, waits for them, and re-layouts: 5 us -> none
    add x1, other arithmetic: 1.53 us -> 3.75 us  [per_device(): return prior_matrix + back.transpose(0, 3, 1, 2, 4).reshape(mine, points)]
    pallas_call x1, Pallas kernels: 74.7 us -> 76.4 us  [analyse(): pl.pallas_call(functools.partial(ensemble_kernel, n, slabs, parts), out_s...]
where the time goes in v1:
time: 80.4 us; the launch traced here: 80.2 us
  Pallas kernels  76.4 us (95%)
  other arithmetic  3.75 us (5%)
    pallas_call x1, Pallas kernels, analyse(): pl.pallas_call(functools.partial(ensemble_kernel, n, slabs, parts), out_s...  76.4 us
    add x1, other arithmetic, per_device(): return prior_matrix + back.transpose(0, 3, 1, 2, 4).reshape(mine, points)  3.75 us

profile of v1, /device:TPU:0, one launch (start us, length us, event | category | flops | bytes accessed | tf_op | source)
XLA Modules:
  0.0 80.2 jit_solution(17528469910342123204)
XLA Ops:
  0.0 76.4 %shard_map.73 = f32[4,16,8,8,128]{4,3,2,1,0:T(8,128)} custom-call(s32[128]{0:T(128)} %totals.1, s32[16,128]{1,0:T(8,128)} %bitcast.9, f32[4,16,8,8,128]{4,3,2,1,0:T(8,128)} %bitcast.7, f32[32,2048]{1,0:T(8,128)} %obs.1, f32[32,2048]{1,0:T(8,128)} %res.1, f32[2,16384]{1,0:T(2,128)} %gxy_all.1, f32[2,8192]{1,0:T(2,128)} %oxy_all.1), custom_call_target="tpu_custom_call" | custom-call | tf_op jit(solution)/shard_map/pallas_call | solution.py:394
  76.4 3.7 %add.3 = f32[32,16384]{1,0:T(8,128)} add(f32[32,16384]{1,0:T(8,128)} %param.7, f32[32,16384]{1,0:T(8,128)} %bitcast.8) | non-fusion elementwise | flops 524288 | bytes 6291456 | tf_op jit(solution)/shard_map/add | solution.py:476

commit v2 on v1

--- a/solution.py
+++ b/solution.py
@@ -295,17 +295,9 @@
         tile = slot * n + region
         found = [numbers[step * GROUP + k, tile] for k in range(GROUP)]
         weights = held[...]
-        both = dot(
-            jnp.concatenate(
-                [
-                    jnp.concatenate([rr[q, :, :TILE] for q in found], axis=1),
-                    jnp.concatenate([rr[q, :, TILE:] for q in found], axis=1),
-                ],
-                axis=0,
-            ),
-            weights,
-        )
-        return both[:members, :TILE] + (both[:members, TILE:] + both[members:, :TILE])
+        both = dot(jnp.concatenate([rr[q, :, :TILE] for q in found], axis=1), weights)
+        rest = dot(jnp.concatenate([rr[q, :, TILE:] for q in found], axis=1), weights[:, :TILE])
+        return both[:, :TILE] + (both[:, TILE:] + rest)
 
     def store(slot, term):
         increment[:, slot] += term.reshape(members // 8, 8, TILE)
@@ -326,11 +318,9 @@
             term = spend(old, before % steps)
             tile = slot * n + region
             made = []
-            listed = [ot[numbers[step * GROUP + k, tile]] for k in range(GROUP)]
-            every = dot(jnp.concatenate(listed, axis=0), ff[slot])
             for k in range(GROUP):
                 p = step * GROUP + k
-                four = every[2 * TILE * k : 2 * TILE * (k + 1)]
+                four = dot(ot[numbers[p, tile]], ff[slot])
                 covariance = four[:TILE, :TILE] + (four[:TILE, TILE:] + four[TILE:, :TILE])
                 made.append(split(tapers[slot * most + p] * covariance))
             for k in range(GROUP):

time: 80.4 us -> 79.2 us (0.985)
  Pallas kernels: 76.4 us -> 75.2 us
    pallas_call x1, Pallas kernels: 76.4 us -> 75.2 us  [analyse(): pl.pallas_call(functools.partial(ensemble_kernel, n, slabs, parts), out_s...]
where the time goes in v2:
time: 79.2 us; the launch traced here: 79 us
  Pallas kernels  75.2 us (95%)
  other arithmetic  3.75 us (5%)
    pallas_call x1, Pallas kernels, analyse(): pl.pallas_call(functools.partial(ensemble_kernel, n, slabs, parts), out_s...  75.2 us
    add x1, other arithmetic, per_device(): return prior_matrix + back.transpose(0, 3, 1, 2, 4).reshape(mine, points)  3.75 us

profile of v2, /device:TPU:0, one launch (start us, length us, event | category | flops | bytes accessed | tf_op | source)
XLA Modules:
  0.0 79.0 jit_solution(14958164463110845235)
XLA Ops:
  0.0 75.2 %shard_map.73 = f32[4,16,8,8,128]{4,3,2,1,0:T(8,128)} custom-call(s32[128]{0:T(128)} %totals.1, s32[16,128]{1,0:T(8,128)} %bitcast.9, f32[4,16,8,8,128]{4,3,2,1,0:T(8,128)} %bitcast.7, f32[32,2048]{1,0:T(8,128)} %obs.1, f32[32,2048]{1,0:T(8,128)} %res.1, f32[2,16384]{1,0:T(2,128)} %gxy_all.1, f32[2,8192]{1,0:T(2,128)} %oxy_all.1), custom_call_target="tpu_custom_call" | custom-call | tf_op jit(solution)/shard_map/pallas_call | solution.py:384
  75.3 3.7 %add.3 = f32[32,16384]{1,0:T(8,128)} add(f32[32,16384]{1,0:T(8,128)} %param.7, f32[32,16384]{1,0:T(8,128)} %bitcast.8) | non-fusion elementwise | flops 524288 | bytes 6291456 | tf_op jit(solution)/shard_map/add | solution.py:466
